TPU v7x, 32 devices: a whole 2x2x4 slice. The times are simulated.
32 devices in a mesh: row: 8 (over y, x, core), col: 4 (over z).
Axes of the slice: x: 2, y: 2, z: 4, core: 2. Of those that a mesh axis runs over, the one named last changes fastest.
Arguments:
- matrix: float32 [16384, 5, 4, 128], P('row', None, 'col'), may hold values from -320 to 320, as said below
Outputs:
- r_rows: float32 [256, 5, 4, 128], P(None, None, 'col')
- residual: float32 [16384, 5, 4, 128], P('row', None, 'col')
Inputs may be any that keep to these rules, and one draw needn't show every extreme that they name: `matrix`: real entries; the first 256 columns have full column rank on every block of 2048 rows.
All inputs are finite; a program needn't handle non-finite values.
Results may differ from a plain program's by a relative error of at most 0.0003.
Values sent between devices are 32-bit elements; how exact they have to be, the bound alone decides.
A program may use at most 128 MiB of HBM per device.

v0:
```python
import math

import jax
import jax.numpy as jnp
from jax import lax
from jax.sharding import PartitionSpec as P


def broadcast(value, axis, root):
    mine = lax.axis_index(axis) == root
    return lax.psum(jnp.where(mine, value, jnp.zeros_like(value)), axis)


def cross_product(left, right):
    return jnp.einsum(
        "mk,mn->kn",
        left,
        right,
        precision=lax.Precision.HIGHEST,
        preferred_element_type=jnp.float32,
    )


def matmul(left, right):
    return jnp.dot(left, right, precision=lax.Precision.HIGHEST, preferred_element_type=jnp.float32)


def factor_pair(gram):
    size = gram.shape[0]
    if size == 1:
        root = jnp.sqrt(gram)
        return (root, 1.0 / root)
    half = size // 2
    first_up, first_inv = factor_pair(gram[:half, :half])
    coupling = cross_product(first_inv, gram[:half, half:])
    schur = gram[half:, half:] - cross_product(coupling, coupling)
    second_up, second_inv = factor_pair(schur)
    lower_zero = jnp.zeros((size - half, half), jnp.float32)
    upper = jnp.concatenate(
        [
            jnp.concatenate([first_up, coupling], axis=1),
            jnp.concatenate([lower_zero, second_up], axis=1),
        ],
        axis=0,
    )
    corner = -matmul(matmul(first_inv, coupling), second_inv)
    inverse = jnp.concatenate(
        [
            jnp.concatenate([first_inv, corner], axis=1),
            jnp.concatenate([lower_zero, second_inv], axis=1),
        ],
        axis=0,
    )
    return (upper, inverse)


def project_after(inverse, panel, local, summed):
    basis_rows = matmul(panel, inverse)
    top = summed(cross_product(basis_rows, local))
    residual = local - matmul(basis_rows, top)
    return (top, residual)


def per_device(matrix):
    rows_here = matrix.shape[0]
    blocks = matrix.shape[1]
    width = matrix.shape[3]
    local = matrix.reshape(rows_here, blocks * width)
    pieces = []
    for owner in range(2):
        pieces.append(broadcast(matrix[:, 0, 0, :], "col", owner))
    panel = jnp.concatenate(pieces, axis=1)
    total_rows = rows_here * lax.axis_size("row")
    gram = cross_product(panel, panel)
    upper, inverse = factor_pair(lax.psum(gram, "row"))

    def summed(value):
        return lax.psum(value, "row")

    top, residual = project_after(inverse, panel, local, summed)
    scaled = top / math.sqrt(total_rows)
    return (
        scaled.reshape(top.shape[0], blocks, 1, width),
        residual.reshape(rows_here, blocks, 1, width),
    )


def solution(mesh):
    return jax.shard_map(
        per_device,
        mesh=mesh,
        in_specs=(P("row", None, "col", None),),
        out_specs=(P(None, None, "col", None), P("row", None, "col", None)),
        check_vma=False,
    )
```

profile of v0, /device:TPU:0, one launch (start us, length us, event | category | flops | bytes accessed | tf_op | source)
XLA Modules:
  0.0 721.3 jit_solution(3593149366638428397)
XLA Ops:
  7.3 3.3 broadcast_select_fusion
  10.6 1.0 select_bitcast_fusion
  11.7 89.9 %all-reduce.136.cloned.1.call-done = (f32[2048,128]{1,0:T(8,128)}, f32[2048,128]{1,0:T(8,128)}) async-done(((f32[2048,128]{1,0:T(8,128)}, f32[2048,128]{1,0:T(8,128)}), (f32[2048,128]{1,0:T(8,128)}, f32[2048,128]{1,0:T(8,128)})) %all-reduce.136.cloned.1.call-update) | async-done | bytes 2097168 | tf_op jit(solution)/shard_map/psum | solution.py:11
  101.6 1.4 constant_dynamic-update-slice_fusion.1
  103.2 4.2 fusion.1342
  107.5 11.7 %copy.264 = f32[2048,5,1,128]{0,3,1,2:T(8,128)} copy(f32[2048,5,1,128]{3,2,1,0:T(1,128)} %param.1) | data formatting | bytes 10485760 | tf_op args[0]
  119.2 40.9 %all-reduce.132.cloned.1.call-done = f32[256,256]{1,0:T(8,128)} async-done(((f32[256,256]{1,0:T(8,128)}), f32[256,256]{1,0:T(8,128)}) %all-reduce.132.cloned.1.call-update) | async-done | bytes 262160 | tf_op jit(solution)/shard_map/psum | solution.py:75
  160.1 1.5 fusion.1214
  164.6 0.9 convolution_subtract_fusion.127
  168.3 1.0 fusion.735
  176.7 1.0 fusion.511
  192.3 1.0 fusion.319
  193.5 0.9 convolution_subtract_fusion.15
  222.4 1.0 fusion.191
  223.7 0.9 convolution_subtract_fusion.7
  619.3 2.0 fusion
  621.3 1.3 copy-done
  622.6 13.2 %fusion.1408 = f32[256,640]{1,0:T(8,128)} fusion(f32[2048,256]{1,0:T(8,128)S(1)} %fusion, f32[2048,640]{0,1:T(8,128)} %bitcast.1420), kind=kOutput, calls=%fused_computation.1806 | convolution fusion | flops 4026531840 | bytes 7995392 | tf_op jit(solution)/shard_map/mk,mn->kn/dot_general | solution.py:15
  635.8 54.6 %all-reduce.134.cloned.1.call-done = f32[256,640]{1,0:T(8,128)} async-done(((f32[256,640]{1,0:T(8,128)}), f32[256,640]{1,0:T(8,128)}) %all-reduce.134.cloned.1.call-update) | async-done | bytes 655376 | tf_op jit(solution)/shard_map/psum | solution.py:78
  690.4 2.0 broadcast_multiply_fusion
  692.4 1.3 copy.265
  693.8 1.1 copy.266
  694.9 7.9 %convolution_subtract_fusion = f32[2048,640]{0,1:T(8,128)} fusion(f32[2048,640]{0,1:T(8,128)} %bitcast.1421, f32[2048,256]{1,0:T(8,128)S(1)} %copy-done.1, f32[256,640]{1,0:T(8,128)S(1)} %copy-done.2), kind=kOutput, calls=%fused_computation | convolution fusion | flops 4027842560 | bytes 13238272 | tf_op jit(solution)/shard_map/dot_general | solution.py:25
  702.8 11.5 %copy.267 = f32[2048,5,1,128]{3,2,1,0:T(1,128)} copy(f32[2048,5,1,128]{0,3,1,2:T(8,128)} %bitcast.1422) | data formatting | bytes 10485760
  (900 shorter events, 201.5 us)
Async XLA Ops:
  7.2 94.4 %all-reduce.136.cloned.1.call-start = ((), (), s32[]{:S(2)}) async-start(), calls=%async_computation.2 | async-start | bytes 4194304 | tf_op jit(solution)/shard_map/psum | solution.py:11
  11.6 148.4 %all-reduce.132.cloned.1.call-start = ((), (), s32[]{:S(2)}) async-start(), calls=%async_computation | async-start | bytes 524288 | tf_op jit(solution)/shard_map/psum | solution.py:75
  101.6 1.5 copy-start.3
  107.4 583.0 %all-reduce.134.cloned.1.call-start = ((), (), s32[]{:S(2)}) async-start(), calls=%async_computation.1 | async-start | bytes 1310720 | tf_op jit(solution)/shard_map/psum | solution.py:78
  160.1 121.7 %copy-start.4 = (f32[256,256]{1,0:T(8,128)S(1)}, f32[256,256]{1,0:T(8,128)}, u32[]{:S(2)}) copy-start(f32[256,256]{1,0:T(8,128)} %all-reduce.132.cloned.1.call-done) | copy-start | bytes 786436
  621.3 1.3 copy-start
  635.8 59.1 %copy-start.1 = (f32[2048,256]{1,0:T(8,128)S(1)}, f32[2048,256]{1,0:T(8,128)}, u32[]{:S(2)}) copy-start(f32[2048,256]{1,0:T(8,128)} %copy-done) | copy-start | bytes 6291460
  690.4 4.5 copy-start.2
Sparse Core Ops, SparseCore 0:
  11.8 89.7 all-reduce.135
  107.5 52.4 all-reduce.131
  635.9 54.4 all-reduce.133
where the time goes:
time: 730 us; the launch traced here: 721 us
  between operations  264 us (36%)
  waiting for transfers between devices  185 us (25%)
  matrix products  130 us (18%)
  local copies, waits for them, and re-layouts  120 us (16%)
  other arithmetic  22 us (3%)
    psum x1, waiting for transfers between devices, broadcast(): return lax.psum(jnp.where(mine, value, jnp.zeros_like(value)), axis)  89.9 us
    slice x128, local copies, waits for them, and re-layouts, factor_pair(): coupling = cross_product(first_inv, gram[:half, half:])  86.2 us
    dot_general x256, matrix products, cross_product(): jnp.einsum('mk,mn->kn', left, right, precision=lax.Precision.HIGHEST, pre...  79.4 us
    psum x1, waiting for transfers between devices, summed(): return lax.psum(value, 'row')  54.6 us
    dot_general x256, matrix products, matmul(): jnp.dot(left, right, precision=lax.Precision.HIGHEST, preferred_element_t...  50.3 us
    psum x1, waiting for transfers between devices, per_device(): upper, inverse = factor_pair(lax.psum(gram, 'row'))  40.9 us
    unnamed x14, local copies, waits for them, and re-layouts  27.2 us
    concatenate x192, other arithmetic, factor_pair(): jnp.concatenate([jnp.concatenate([first_inv, corner], axis=1), jnp.concat...  15.7 us
  transfers between devices with their start and end apart: 3, of which 3 were waited for; matrix products, arithmetic and copies ran while one was open for 2% of the time, Pallas kernels for 0%

commit v1 on v0

v1 whole, which is shorter than its diff:
```python
import functools
import math

import jax
import jax.numpy as jnp
from jax import lax
from jax.experimental import pallas as pl
from jax.experimental.pallas import tpu as pltpu
from jax.sharding import PartitionSpec as P

VMEM_LIMIT = 48 * 1024 * 1024
LANES = 128


def dot_exact(left, right, contract_left, contract_right):
    return lax.dot_general(
        left,
        right,
        (((contract_left,), (contract_right,)), ((), ())),
        precision=lax.Precision.HIGHEST,
        preferred_element_type=jnp.float32,
    )


def split(value):
    high = value.astype(jnp.bfloat16)
    low = (value - high.astype(jnp.float32)).astype(jnp.bfloat16)
    return high, low


def dot_split(left, right):
    left_high, left_low = left
    right_high, right_low = right
    dot = functools.partial(jnp.dot, preferred_element_type=jnp.float32)
    return dot(left_high, right_high) + (dot(left_high, right_low) + dot(left_low, right_high))


def lower_inverse(block):
    size = block.shape[0]
    row = lax.broadcasted_iota(jnp.int32, (size, 1), 0)
    row8 = lax.broadcasted_iota(jnp.int32, (8, 1), 0)
    eye = (
        lax.broadcasted_iota(jnp.int32, (size, size), 0)
        == lax.broadcasted_iota(jnp.int32, (size, size), 1)
    ).astype(jnp.float32)

    def group(step, carry):
        left, right = carry
        limit = size - 8 * step
        for j in range(8):
            pivot = left[j : j + 1, j : j + 1]
            root = lax.rsqrt(pivot)
            root = root * (1.5 - 0.5 * (pivot * root) * root)
            left_row = left[j : j + 1, :] * root
            right_row = right[j : j + 1, :] * root
            factor = jnp.where((row > j) & (row < limit), left[:, j : j + 1] * root, 0.0)
            left = left - factor * left_row
            right = right - factor * right_row
            head = jnp.where(row8 == j, right_row, right[:8])
            right = jnp.concatenate([head, right[8:]], axis=0)
        left = jnp.concatenate([left[8:], left[:8]], axis=0)
        left = pltpu.roll(left, size - 8, 1)
        right = jnp.concatenate([right[8:], right[:8]], axis=0)
        return left, right

    return lax.fori_loop(0, size // 8, group, (block, eye))[1]


def factor_into(top_left, top_right, bottom_right, out_ref):
    first = lower_inverse(top_left)
    coupling = dot_exact(first, top_right, 1, 0)
    schur = bottom_right - dot_exact(coupling, coupling, 0, 0)
    second = lower_inverse(schur)
    corner = -dot_exact(second, dot_exact(coupling, first, 0, 0), 1, 0)
    half = top_left.shape[0]
    out_ref[:half, :half] = first
    out_ref[:half, half:] = jnp.zeros_like(first)
    out_ref[half:, :half] = corner
    out_ref[half:, half:] = second


def update_kernel(
    scale, chunk, matrix, panel, summed, inverse, r_rows, residual,
    local, wide, result, top_buf, load_sem, panel_sem, store_sem, top_sem,
):
    rows = matrix.shape[0]
    blocks = matrix.shape[1]
    count = rows // chunk

    def span(c):
        return pl.ds(c * chunk, chunk)

    def load(c, b):
        return pltpu.make_async_copy(
            matrix.at[span(c), b, 0, :], local.at[b, span(c), :], load_sem.at[c, b]
        )

    def load_panel(c, h):
        return pltpu.make_async_copy(
            panel.at[h, span(c), :], wide.at[h, span(c), :], panel_sem.at[c, h]
        )

    def store(c, b):
        return pltpu.make_async_copy(
            result.at[b, span(c), :], residual.at[span(c), b, 0, :], store_sem.at[c, b]
        )

    def store_top(b):
        return pltpu.make_async_copy(top_buf.at[b], r_rows.at[:, b, 0, :], top_sem.at[b])

    for c in range(count):
        for h in range(2):
            load_panel(c, h).start()
        for b in range(blocks):
            load(c, b).start()
    top = dot_exact(inverse[...], summed[...], 1, 0)
    for b in range(blocks):
        top_buf[b] = top[:, b * LANES : (b + 1) * LANES] * scale
        store_top(b).start()
    weights = split(dot_exact(inverse[...], top, 0, 0))
    for c in range(count):
        for h in range(2):
            load_panel(c, h).wait()
        for b in range(blocks):
            load(c, b).wait()
        rows_c = slice(c * chunk, (c + 1) * chunk)
        left = split(jnp.concatenate([wide[0, rows_c, :], wide[1, rows_c, :]], axis=1))
        product = dot_split(left, weights)
        for b in range(blocks):
            result[b, rows_c, :] = local[b, rows_c, :] - product[:, b * LANES : (b + 1) * LANES]
            store(c, b).start()
    for b in range(blocks):
        store_top(b).wait()
        for c in range(count):
            store(c, b).wait()


def update(matrix, panel, summed, inverse, total_rows):
    rows, blocks, _, width = matrix.shape
    chunk = 256
    count = rows // chunk
    names = pltpu.SemaphoreType.DMA
    vmem = pl.BlockSpec(memory_space=pltpu.VMEM)
    hbm = pl.BlockSpec(memory_space=pl.ANY)
    return pl.pallas_call(
        functools.partial(update_kernel, 1.0 / math.sqrt(total_rows), chunk),
        out_shape=(
            jax.ShapeDtypeStruct((2 * width, blocks, 1, width), jnp.float32),
            jax.ShapeDtypeStruct(matrix.shape, jnp.float32),
        ),
        in_specs=[hbm, hbm, vmem, vmem],
        out_specs=(hbm, hbm),
        scratch_shapes=[
            pltpu.VMEM((blocks, rows, width), jnp.float32),
            pltpu.VMEM((2, rows, width), jnp.float32),
            pltpu.VMEM((blocks, rows, width), jnp.float32),
            pltpu.VMEM((blocks, 2 * width, width), jnp.float32),
            names((count, blocks)),
            names((count, 2)),
            names((count, blocks)),
            names((blocks,)),
        ],
        compiler_params=pltpu.CompilerParams(vmem_limit_bytes=VMEM_LIMIT),
        name="update",
    )(matrix, panel, summed, inverse)


def factor_kernel(gram, out):
    factor_into(
        gram[:LANES, :LANES], gram[:LANES, LANES:], gram[LANES:, LANES:], out
    )


def factor(gram):
    vmem = pl.BlockSpec(memory_space=pltpu.VMEM)
    return pl.pallas_call(
        factor_kernel,
        out_shape=jax.ShapeDtypeStruct(gram.shape, jnp.float32),
        in_specs=[vmem],
        out_specs=vmem,
        compiler_params=pltpu.CompilerParams(vmem_limit_bytes=VMEM_LIMIT),
        name="factor",
    )(gram)


def per_device(matrix):
    rows, blocks, _, width = matrix.shape
    me = lax.axis_index("col")
    n_col = lax.axis_size("col")
    own = matrix[:, 0, 0, :]
    chain = [(i, i + 1) for i in range(n_col - 1)]
    back = lax.ppermute(own, "col", [(1, 0)])
    first = second = own
    first = jnp.where(me == 1, back, own)
    second = jnp.where(me == 0, back, own)
    moving = own
    for step in range(1, n_col):
        moving = lax.ppermute(moving, "col", chain)
        first = jnp.where(me == step, moving, first)
        second = jnp.where(me == step + 1, moving, second)
    panel = jnp.stack([first, second])
    pair = jnp.concatenate([first, second], axis=1)
    local = matrix.reshape(rows, blocks * width)
    both = dot_exact(pair, jnp.concatenate([pair, local], axis=1), 0, 0)
    both = lax.psum(both, "row")
    inverse = factor(both[:, : 2 * width])
    total_rows = rows * lax.axis_size("row")
    return update(matrix, panel, both[:, 2 * width :], inverse, total_rows)


def solution(mesh):
    return jax.shard_map(
        per_device,
        mesh=mesh,
        in_specs=(P("row", None, "col", None),),
        out_specs=(P(None, None, "col", None), P("row", None, "col", None)),
        check_vma=False,
    )
```

time: 730 us -> 202 us (0.28); the launches traced: 721 us -> 202 us
  between operations: 264 us -> 14.2 us
  matrix products: 130 us -> 8.25 us
  local copies, waits for them, and re-layouts: 120 us -> 9.17 us
  waiting for transfers between devices: 185 us -> 97.1 us
  Pallas kernels: 0 us -> 36.5 us
  starting transfers between devices: 0.12 us -> 16.2 us
    psum x3 -> x1, waiting for transfers between devices: 185 us -> 54.6 us  [per_device(): both = lax.psum(both, 'row')]
    dot_general x512 -> x1, matrix products: 130 us -> 8.25 us  [dot_exact(): lax.dot_general(left, right, (((contract_left,), (contract_right,)), ((),...]
    slice x128 -> x3, local copies, waits for them, and re-layouts: 86.2 us -> 3.36 us  [the longest x1 1.26 us: per_device(): own = matrix[:, 0, 0, :]]
    ppermute x0 -> x4, waiting for transfers between devices: none -> 42.5 us  [the longest x3 42.5 us: per_device(): moving = lax.ppermute(moving, 'col', chain)]
    pallas_call x0 -> x2, Pallas kernels: none -> 36.5 us  [the longest x1 26.1 us: factor(): pl.pallas_call(factor_kernel, out_shape=jax.ShapeDtypeStruct(gram.shape,...]
    unnamed x14 -> x11, local copies, waits for them, and re-layouts: 27.2 us -> 5.81 us
    unnamed x0 -> x1, other arithmetic: none -> 17.1 us
    ppermute x0 -> x4, starting transfers between devices: none -> 16.2 us  [the longest x3 14.9 us: per_device(): moving = lax.ppermute(moving, 'col', chain)]
  transfers between devices with their start and end apart: 3 -> 5, of which waited for: 3 -> 3; matrix products, arithmetic and copies ran while one was open for 2% -> 12% of each run, Pallas kernels for 0% -> 0%
where the time goes in v1:
time: 202 us
  waiting for transfers between devices  97.1 us (48%)
  Pallas kernels  36.5 us (18%)
  other arithmetic  20.3 us (10%)
  starting transfers between devices  16.2 us (8%)
  between operations  14.2 us (7%)
  local copies, waits for them, and re-layouts  9.17 us (5%)
  matrix products  8.25 us (4%)
    psum x1, waiting for transfers between devices, per_device(): both = lax.psum(both, 'row')  54.6 us
    ppermute x3, waiting for transfers between devices, per_device(): moving = lax.ppermute(moving, 'col', chain)  42.5 us
    pallas_call x1, Pallas kernels, factor(): pl.pallas_call(factor_kernel, out_shape=jax.ShapeDtypeStruct(gram.shape,...  26.1 us
    unnamed x1, other arithmetic  17.1 us
    ppermute x3, starting transfers between devices, per_device(): moving = lax.ppermute(moving, 'col', chain)  14.9 us
    pallas_call x1, Pallas kernels, update(): pl.pallas_call(functools.partial(update_kernel, 1.0 / math.sqrt(total_row...  10.4 us
    dot_general x1, matrix products, dot_exact(): lax.dot_general(left, right, (((contract_left,), (contract_right,)), ((),...  8.25 us
    unnamed x11, local copies, waits for them, and re-layouts  5.81 us
  transfers between devices with their start and end apart: 5, of which 3 were waited for; matrix products, arithmetic and copies ran while one was open for 12% of the time, Pallas kernels for 0%

profile of v1, /device:TPU:0, one launch (start us, length us, event | category | flops | bytes accessed | tf_op | source)
XLA Modules:
  0.0 201.6 jit_solution(12222780184275400231)
XLA Ops:
  7.2 0.0 all-reduce.2.cloned.1.call-start
  7.2 1.3 slice.9
  8.5 5.0 %collective-permute-start = (f32[2048,128]{1,0:T(8,128)S(1)}, f32[2048,128]{1,0:T(8,128)S(1)}, u32[]{:S(2)}, u32[]{:S(2)}) collective-permute-start(f32[2048,128]{1,0:T(8,128)S(1)} %bitcast.11), channel_id=1, source_target_pairs={{0,1},{1,2},{2,3},{4,5},{5,6},{6,7},{8,9},{9,10},{10,11},{12,13},{... | collective-permute-start | bytes 3145736 | tf_op jit(solution)/shard_map/ppermute | solution.py:198
  13.5 22.3 %collective-permute-done = f32[2048,128]{1,0:T(8,128)S(1)} collective-permute-done((f32[2048,128]{1,0:T(8,128)S(1)}, f32[2048,128]{1,0:T(8,128)S(1)}, u32[]{:S(2)}, u32[]{:S(2)}) %collective-permute-start) | collective-permute-done | bytes 1048608 | tf_op jit(solution)/shard_map/ppermute | solution.py:198
  35.8 1.0 copy-done.1
  36.8 4.4 %collective-permute-start.1 = (f32[2048,128]{1,0:T(8,128)S(1)}, f32[2048,128]{1,0:T(8,128)S(1)}, u32[]{:S(2)}, u32[]{:S(2)}) collective-permute-start(f32[2048,128]{1,0:T(8,128)S(1)} %collective-permute-done), channel_id=1, source_target_pairs={{0,1},{1,2},{2,3},{4,5},{5,6},{6,7},{8,9},{9,10},{10,11},{12,13},{... | collective-permute-start | bytes 3145736 | tf_op jit(solution)/shard_map/ppermute | solution.py:198
  41.2 1.3 collective-permute-start.3
  42.5 20.2 %collective-permute-done.1 = f32[2048,128]{1,0:T(8,128)S(1)} collective-permute-done((f32[2048,128]{1,0:T(8,128)S(1)}, f32[2048,128]{1,0:T(8,128)S(1)}, u32[]{:S(2)}, u32[]{:S(2)}) %collective-permute-start.1) | collective-permute-done | bytes 1048608 | tf_op jit(solution)/shard_map/ppermute | solution.py:198
  62.7 5.4 %collective-permute-start.2 = (f32[2048,128]{1,0:T(8,128)S(1)}, f32[2048,128]{1,0:T(8,128)}, u32[]{:S(2)}, u32[]{:S(2)}) collective-permute-start(f32[2048,128]{1,0:T(8,128)S(1)} %collective-permute-done.1), channel_id=1, source_target_pairs={{0,1},{1,2},{2,3},{4,5},{5,6},{6,7},{8,9},{9,10},{10,11},{12,13},{... | collective-permute-start | bytes 3145736 | tf_op jit(solution)/shard_map/ppermute | solution.py:198
  68.1 17.1 %reduce = f32[2048,5,128]{2,1,0:T(8,128)} reduce(f32[2048,5,1,128]{3,2,1,0:T(1,128)} %matrix.1, f32[]{:T(128)} %constant.15), dimensions={2}, to_apply=%param.1.reduce_sub_computation | reduce | bytes 10485764 | tf_op args[0]
  85.2 0.0 copy-done.3
  85.2 4.8 %copy.7 = f32[256,8,5,128]{3,1,2,0:T(8,128)S(1)} copy(f32[256,8,5,128]{3,2,1,0:T(8,128)} %bitcast.9) | data formatting | bytes 10485760
  90.0 0.0 collective-permute-done.3
  90.0 0.0 collective-permute-done.2
  90.1 1.8 select_select_fusion.1
  91.9 0.0 copy-start
  91.9 8.2 %fusion = f32[256,896]{1,0:T(8,128)} fusion(f32[2048,640]{1,0:T(8,128)S(1)} %bitcast.10, f32[2048,128]{1,0:T(8,128)S(1)} %get-tuple-element.3, f32[2048,128]{1,0:T(8,128)S(1)} %get-tuple-element.2), kind=kOutput, calls=%fused_computation | convolution fusion | flops 5641338880 | bytes 8257536 | tf_op jit(solution)/shard_map/dot_general | solution.py:16
  100.2 0.0 all-reduce.2.cloned.1.call-update
  100.2 1.4 pad_maximum_fusion.panel
  101.6 54.6 %all-reduce.2.cloned.1.call-done = f32[256,896]{1,0:T(8,128)} async-done(((f32[256,896]{1,0:T(8,128)}), f32[256,896]{1,0:T(8,128)}) %all-reduce.2.cloned.1.call-update) | async-done | bytes 917520 | tf_op jit(solution)/shard_map/psum | solution.py:205
  156.2 1.0 slice.13.gram
  157.2 26.1 %factor.1.inverse = f32[256,256]{1,0:T(8,128)S(1)} custom-call(f32[256,256]{1,0:T(8,128)S(1)} %slice.13.gram), custom_call_target="tpu_custom_call" | custom-call | tf_op jit(solution)/shard_map/factor/pallas_call | solution.py:176
  183.2 1.1 slice.12.summed
  184.4 10.4 %update.1 = (f32[256,5,1,128]{3,2,1,0:T(1,128)}, f32[2048,5,1,128]{3,2,1,0:T(1,128)}) custom-call(f32[2048,5,1,128]{3,2,1,0:T(1,128)} %matrix.1, f32[2,2048,128]{2,1,0:T(8,128)S(1)} %pad_maximum_fusion.panel, f32[256,640]{1,0:T(8,128)S(1)} %slice.12.summed, f32[256,256]{1,0:T(8,128)S(1)} %factor.1.inverse), custom_call_target="tpu_custom_call" | custom-call | tf_op jit(solution)/shard_map/update/pallas_call | solution.py:145
  (7 shorter events, 0.0 us)
Async XLA Ops:
  7.2 149.0 %all-reduce.2.cloned.1.call-start = ((), (), s32[]{:S(2)}) async-start(), calls=%async_computation | async-start | bytes 1835008 | tf_op jit(solution)/shard_map/psum | solution.py:205
  8.5 27.3 %collective-permute-start = (f32[2048,128]{1,0:T(8,128)S(1)}, f32[2048,128]{1,0:T(8,128)S(1)}, u32[]{:S(2)}, u32[]{:S(2)}) collective-permute-start(f32[2048,128]{1,0:T(8,128)S(1)} %bitcast.11), channel_id=1, source_target_pairs={{0,1},{1,2},{2,3},{4,5},{5,6},{6,7},{8,9},{9,10},{10,11},{12,13},{... | collective-permute-start | bytes 3145736 | tf_op jit(solution)/shard_map/ppermute | solution.py:198
  35.8 1.0 copy-start.1
  36.8 25.9 %collective-permute-start.1 = (f32[2048,128]{1,0:T(8,128)S(1)}, f32[2048,128]{1,0:T(8,128)S(1)}, u32[]{:S(2)}, u32[]{:S(2)}) collective-permute-start(f32[2048,128]{1,0:T(8,128)S(1)} %collective-permute-done), channel_id=1, source_target_pairs={{0,1},{1,2},{2,3},{4,5},{5,6},{6,7},{8,9},{9,10},{10,11},{12,13},{... | collective-permute-start | bytes 3145736 | tf_op jit(solution)/shard_map/ppermute | solution.py:198
  41.2 48.8 %collective-permute-start.3 = (f32[2048,128]{1,0:T(8,128)S(1)}, f32[2048,128]{1,0:T(8,128)}, u32[]{:S(2)}, u32[]{:S(2)}) collective-permute-start(f32[2048,128]{1,0:T(8,128)S(1)} %bitcast.12), channel_id=1, source_target_pairs={{1,0},{5,4},{9,8},{13,12},{17,16},{21,20},{25,24},{29,28}} | collective-permute-start | bytes 3145736 | tf_op jit(solution)/shard_map/ppermute | solution.py:192
  62.7 22.5 %copy-start.3 = (f32[2048,128]{1,0:T(8,128)}, f32[2048,128]{1,0:T(8,128)S(1)}, u32[]{:S(2)}) copy-start(f32[2048,128]{1,0:T(8,128)S(1)} %collective-permute-done.1) | copy-start | bytes 3145732
  62.7 27.4 %collective-permute-start.2 = (f32[2048,128]{1,0:T(8,128)S(1)}, f32[2048,128]{1,0:T(8,128)}, u32[]{:S(2)}, u32[]{:S(2)}) collective-permute-start(f32[2048,128]{1,0:T(8,128)S(1)} %collective-permute-done.1), channel_id=1, source_target_pairs={{0,1},{1,2},{2,3},{4,5},{5,6},{6,7},{8,9},{9,10},{10,11},{12,13},{... | collective-permute-start | bytes 3145736 | tf_op jit(solution)/shard_map/ppermute | solution.py:198
  85.2 4.9 %copy-start.2 = (f32[2048,128]{1,0:T(8,128)S(1)}, f32[2048,128]{1,0:T(8,128)}, u32[]{:S(2)}) copy-start(f32[2048,128]{1,0:T(8,128)} %copy-done.1) | copy-start | bytes 3145732
  85.2 4.9 %copy-start.4 = (f32[2048,128]{1,0:T(8,128)S(1)}, f32[2048,128]{1,0:T(8,128)}, u32[]{:S(2)}) copy-start(f32[2048,128]{1,0:T(8,128)} %copy-done.3) | copy-start | bytes 3145732
  91.9 8.3 %copy-start = (f32[2048,128]{1,0:T(8,128)}, f32[2048,128]{1,0:T(8,128)S(1)}, u32[]{:S(2)}) copy-start(f32[2048,128]{1,0:T(8,128)S(1)} %get-tuple-element.3) | copy-start | bytes 3145732
Sparse Core Ops, SparseCore 0:
  100.3 55.8 all-reduce.1

commit v2 on v1

--- a/solution.py
+++ b/solution.py
@@ -64,19 +64,6 @@
         return left, right
 
     return lax.fori_loop(0, size // 8, group, (block, eye))[1]
-
-
-def factor_into(top_left, top_right, bottom_right, out_ref):
-    first = lower_inverse(top_left)
-    coupling = dot_exact(first, top_right, 1, 0)
-    schur = bottom_right - dot_exact(coupling, coupling, 0, 0)
-    second = lower_inverse(schur)
-    corner = -dot_exact(second, dot_exact(coupling, first, 0, 0), 1, 0)
-    half = top_left.shape[0]
-    out_ref[:half, :half] = first
-    out_ref[:half, half:] = jnp.zeros_like(first)
-    out_ref[half:, :half] = corner
-    out_ref[half:, half:] = second
 
 
 def update_kernel(
@@ -164,48 +151,349 @@
         name="update",
     )(matrix, panel, summed, inverse)
 
-
-def factor_kernel(gram, out):
-    factor_into(
-        gram[:LANES, :LANES], gram[:LANES, LANES:], gram[LANES:, LANES:], out
-    )
-
-
-def factor(gram):
+def stream_kernel(
+    n_row, n_col, owners, chunk, matrix, panel, summed, inverse,
+    local, wide, work, total, gram, gram_total, slots, gram_slots, factors,
+    load_sem, own_sem, out_sem, recv_sem, send_sem, factor_recv, factor_send,
+    scatter_send, scatter_recv, gather_send, gather_recv,
+):
+    rows, blocks = matrix.shape[0], matrix.shape[1]
+    count = rows // chunk
+    piece = LANES // owners
+    row = lax.axis_index("row")
+    col = lax.axis_index("col")
+    has_right = col < n_col - 1
+
+    def span(c):
+        return pl.ds(pl.multiple_of(c * chunk, chunk), chunk)
+
+    def remote(source, target, sent, received, to_row, to_col):
+        return pltpu.make_async_remote_copy(
+            src_ref=source,
+            dst_ref=target,
+            send_sem=sent,
+            recv_sem=received,
+            device_id={"row": to_row, "col": to_col},
+            device_id_type=pl.DeviceIdType.MESH,
+        )
+
+    def send(way, half, c):
+        place = wide.at[half, span(c), :]
+        to_col = col + 1 if way == 0 else col - 1
+        return remote(
+            place, place, send_sem.at[way, half, c], recv_sem.at[half, c], row, to_col
+        )
+
+    def send_factor(which):
+        place = factors.at[which]
+        return remote(
+            place, place, factor_send.at[which], factor_recv.at[which], row, col + 1
+        )
+
+    def load(b):
+        return pltpu.make_async_copy(matrix.at[:, b, 0, :], local.at[b], load_sem.at[b])
+
+    def load_own(half):
+        return pltpu.make_async_copy(matrix.at[:, 0, 0, :], wide.at[half], own_sem)
+
+    def store_panel(half):
+        return pltpu.make_async_copy(wide.at[half], panel.at[half], out_sem.at[half])
+
+    def source_of(stage, owner):
+        start = pl.multiple_of(owner * piece, 8)
+        if stage == 2:
+            return gram.at[pl.ds(start, piece), :]
+        return work.at[pl.ds(stage * LANES + start, piece), :]
+
+    def total_of(stage, owner):
+        start = pl.multiple_of(owner * piece, 8)
+        if stage == 2:
+            return gram_total.at[pl.ds(start, piece), :]
+        return total.at[pl.ds(stage * LANES + start, piece), :]
+
+    def slot_of(stage, d):
+        return gram_slots.at[d] if stage == 2 else slots.at[stage, d]
+
+    def scatter(stage, d):
+        owner = lax.rem(row + d, n_row)
+        copy = remote(
+            source_of(stage, owner), slot_of(stage, d),
+            scatter_send.at[stage, d], scatter_recv.at[stage, d], owner, col,
+        )
+        return owner, copy
+
+    def gather(stage, d):
+        other = lax.rem(row + d, n_row)
+        place = total_of(stage, row)
+        return remote(
+            place, place, gather_send.at[stage, d], gather_recv.at[stage, d], other, col
+        )
+
+    def scatter_start(stage):
+        @pl.loop(1, n_row)
+        def _(d):
+            owner, copy = scatter(stage, d)
+            pl.when(owner < owners)(copy.start)
+
+    def scatter_finish(stage):
+        @pl.when(row < owners)
+        def _():
+            @pl.loop(1, n_row)
+            def _(d):
+                slot = slot_of(stage, d)
+                remote(
+                    slot, slot, scatter_send.at[stage, d], scatter_recv.at[stage, d], row, col
+                ).wait_recv()
+
+            value = source_of(stage, row)[...]
+            for d in range(1, n_row):
+                value = value + slot_of(stage, d)[...]
+            total_of(stage, row)[...] = value
+
+            @pl.loop(1, n_row)
+            def _(d):
+                gather(stage, d).start()
+
+    def gather_finish(stage):
+        @pl.loop(1, n_row)
+        def _(d):
+            other = lax.rem(row - d + n_row, n_row)
+
+            @pl.when(other < owners)
+            def _():
+                place = total_of(stage, other)
+                remote(
+                    place, place, gather_send.at[stage, d], gather_recv.at[stage, d], row, col
+                ).wait_recv()
+
+    def settle(stage):
+        @pl.loop(1, n_row)
+        def _(d):
+            owner, copy = scatter(stage, d)
+            pl.when(owner < owners)(copy.wait_send)
+            pl.when(row < owners)(gather(stage, d).wait_send)
+
+    def window(c):
+        return jnp.concatenate([local[b, span(c), :] for b in range(blocks)], axis=1)
+
+    for half in range(2):
+        pl.when(col == half)(load_own(half).start)
+    for b in range(blocks):
+        load(b).start()
+
+    barrier = pltpu.get_barrier_semaphore()
+
+    def greet(to_row, to_col):
+        pl.semaphore_signal(
+            barrier,
+            inc=1,
+            device_id={"row": to_row, "col": to_col},
+            device_id_type=pl.DeviceIdType.MESH,
+        )
+
+    for d in range(1, n_row):
+        greet(lax.rem(row + d, n_row), col)
+    pl.when(col > 0)(lambda: greet(row, col - 1))
+    pl.when(has_right)(lambda: greet(row, col + 1))
+    work[...] = jnp.zeros_like(work)
+    gram[...] = jnp.zeros_like(gram)
+    inner = (col > 0) & has_right
+    pl.semaphore_wait(barrier, n_row + inner.astype(jnp.int32))
+
+    @pl.when(col < 2)
+    def _():
+        load_own(0).wait()
+
+    @pl.when(col == 0)
+    def _():
+        @pl.loop(0, count)
+        def _(c):
+            send(0, 0, c).start()
+
+    @pl.when(col == 1)
+    def _():
+        @pl.loop(0, count)
+        def _(c):
+            if n_col > 2:
+                send(0, 1, c).start()
+            send(1, 1, c).start()
+
+    for b in range(blocks):
+        load(b).wait()
+
+    @pl.when(col < 2)
+    def _():
+        @pl.loop(0, count)
+        def _(c):
+            send(0, 1 - col, c).wait_recv()
+
+            if n_col > 2:
+
+                @pl.when((col == 1) & (c >= count // 2))
+                def _():
+                    send(0, 0, 2 * c - count).start()
+                    send(0, 0, 2 * c - count + 1).start()
+
+            pair = jnp.concatenate([wide[0, span(c), :], wide[1, span(c), :]], axis=1)
+            cross = dot_exact(pair, pair, 0, 0)
+            gram[...] += jnp.concatenate([cross[:LANES], cross[LANES:]], axis=1)
+            work[...] += dot_exact(pair, window(c), 0, 0)
+
+        scatter_start(2)
+        for half in range(2):
+            store_panel(half).start()
+        scatter_start(1)
+        scatter_finish(2)
+        scatter_start(0)
+        gather_finish(2)
+        first = lower_inverse(gram_total[:, :LANES])
+        factors[0] = first
+
+        if n_col > 2:
+            pl.when(col == 1)(send_factor(0).start)
+        coupling = dot_exact(first, gram_total[:, LANES : 2 * LANES], 1, 0)
+        schur = gram_total[:, 3 * LANES :] - dot_exact(coupling, coupling, 0, 0)
+        carried = dot_exact(coupling, first, 0, 0)
+        second = lower_inverse(schur)
+        factors[1] = second
+        if n_col > 2:
+            pl.when(col == 1)(send_factor(1).start)
+        factors[2] = -dot_exact(second, carried, 1, 0)
+        if n_col > 2:
+            pl.when(col == 1)(send_factor(2).start)
+        scatter_finish(1)
+        scatter_finish(0)
+        gather_finish(1)
+        gather_finish(0)
+        for half in range(2):
+            store_panel(half).wait()
+        for stage in (2, 1, 0):
+            settle(stage)
+
+        @pl.loop(0, count)
+        def _(c):
+            @pl.when(col == 0)
+            def _():
+                send(0, 0, c).wait_send()
+
+            @pl.when(col == 1)
+            def _():
+                send(1, 1, c).wait_send()
+                if n_col > 2:
+                    send(0, 1, c).wait_send()
+                    send(0, 0, c).wait_send()
+
+        if n_col > 2:
+
+            @pl.when(col == 1)
+            def _():
+                for which in range(3):
+                    send_factor(which).wait_send()
+
+    if n_col > 2:
+
+        @pl.when(col >= 2)
+        def _():
+            for half in (1, 0):
+
+                @pl.loop(0, count)
+                def _(c):
+                    send(0, half, c).wait_recv()
+                    pl.when(has_right)(send(0, half, c).start)
+                    if half == 0:
+                        pl.when(c == count // 2)(lambda: scatter_finish(1))
+                    here = pl.ds(half * LANES, LANES)
+                    work[here, :] += dot_exact(wide[half, span(c), :], window(c), 0, 0)
+
+                scatter_start(half)
+                store_panel(half).start()
+
+            scatter_finish(0)
+            for which in range(3):
+                send_factor(which).wait_recv()
+                pl.when(has_right)(send_factor(which).start)
+            gather_finish(1)
+            gather_finish(0)
+            for half in range(2):
+                store_panel(half).wait()
+            for stage in (1, 0):
+                settle(stage)
+
+            @pl.when(has_right)
+            def _():
+                @pl.loop(0, count)
+                def _(c):
+                    for half in range(2):
+                        send(0, half, c).wait_send()
+
+                for which in range(3):
+                    send_factor(which).wait_send()
+
+    summed[...] = total[...]
+    inverse[:LANES, :LANES] = factors[0]
+    inverse[:LANES, LANES:] = jnp.zeros((LANES, LANES), jnp.float32)
+    inverse[LANES:, :LANES] = factors[2]
+    inverse[LANES:, LANES:] = factors[1]
+
+
+def stream(matrix):
+    rows, blocks, _, width = matrix.shape
+    n_row = lax.axis_size("row")
+    n_col = lax.axis_size("col")
+    owners = min(n_row, 16)
+    piece = LANES // owners
+    chunk = 256
+    count = rows // chunk
+    columns = blocks * width
+    sem = pltpu.SemaphoreType.DMA
     vmem = pl.BlockSpec(memory_space=pltpu.VMEM)
+    hbm = pl.BlockSpec(memory_space=pl.ANY)
+
+    def floats(*shape):
+        return pltpu.VMEM(shape, jnp.float32)
+
     return pl.pallas_call(
-        factor_kernel,
-        out_shape=jax.ShapeDtypeStruct(gram.shape, jnp.float32),
-        in_specs=[vmem],
-        out_specs=vmem,
-        compiler_params=pltpu.CompilerParams(vmem_limit_bytes=VMEM_LIMIT),
-        name="factor",
-    )(gram)
+        functools.partial(stream_kernel, n_row, n_col, owners, chunk),
+        out_shape=(
+            jax.ShapeDtypeStruct((2, rows, width), jnp.float32),
+            jax.ShapeDtypeStruct((2 * width, columns), jnp.float32),
+            jax.ShapeDtypeStruct((2 * width, 2 * width), jnp.float32),
+        ),
+        in_specs=[hbm],
+        out_specs=(hbm, vmem, vmem),
+        scratch_shapes=[
+            floats(blocks, rows, width),
+            floats(2, rows, width),
+            floats(2 * width, columns),
+            floats(2 * width, columns),
+            floats(width, 4 * width),
+            floats(width, 4 * width),
+            floats(2, n_row, piece, columns),
+            floats(n_row, piece, 4 * width),
+            floats(3, width, width),
+            sem((blocks,)),
+            sem,
+            sem((2,)),
+            sem((2, count)),
+            sem((2, 2, count)),
+            sem((3,)),
+            sem((3,)),
+            sem((3, n_row)),
+            sem((3, n_row)),
+            sem((3, n_row)),
+            sem((3, n_row)),
+        ],
+        compiler_params=pltpu.CompilerParams(
+            collective_id=0, has_side_effects=True, vmem_limit_bytes=VMEM_LIMIT
+        ),
+        name="stream",
+    )(matrix)
 
 
 def per_device(matrix):
-    rows, blocks, _, width = matrix.shape
-    me = lax.axis_index("col")
-    n_col = lax.axis_size("col")
-    own = matrix[:, 0, 0, :]
-    chain = [(i, i + 1) for i in range(n_col - 1)]
-    back = lax.ppermute(own, "col", [(1, 0)])
-    first = second = own
-    first = jnp.where(me == 1, back, own)
-    second = jnp.where(me == 0, back, own)
-    moving = own
-    for step in range(1, n_col):
-        moving = lax.ppermute(moving, "col", chain)
-        first = jnp.where(me == step, moving, first)
-        second = jnp.where(me == step + 1, moving, second)
-    panel = jnp.stack([first, second])
-    pair = jnp.concatenate([first, second], axis=1)
-    local = matrix.reshape(rows, blocks * width)
-    both = dot_exact(pair, jnp.concatenate([pair, local], axis=1), 0, 0)
-    both = lax.psum(both, "row")
-    inverse = factor(both[:, : 2 * width])
-    total_rows = rows * lax.axis_size("row")
-    return update(matrix, panel, both[:, 2 * width :], inverse, total_rows)
+    panel, summed, inverse = stream(matrix)
+    total_rows = matrix.shape[0] * lax.axis_size("row")
+    return update(matrix, panel, summed, inverse, total_rows)
 
 
 def solution(mesh):

time: 202 us -> 88.3 us (0.44)
  waiting for transfers between devices: 97.1 us -> 0 us
  Pallas kernels: 36.5 us -> 87.5 us
  other arithmetic: 20.3 us -> 0 us
  starting transfers between devices: 16.2 us -> 0 us
  between operations: 14.2 us -> 0.64 us
  local copies, waits for them, and re-layouts: 9.17 us -> 0 us
  matrix products: 8.25 us -> 0 us
    psum x1 -> x0, waiting for transfers between devices: 54.6 us -> none  [per_device(): both = lax.psum(both, 'row')]
    pallas_call x1, Pallas kernels: 26.1 us -> 77.3 us  [stream(): pl.pallas_call(functools.partial(stream_kernel, n_row, n_col, owners, chu...]
    ppermute x4 -> x0, waiting for transfers between devices: 42.5 us -> none  [the longest x3 42.5 us: per_device(): moving = lax.ppermute(moving, 'col', chain)]
    unnamed x1 -> x0, other arithmetic: 17.1 us -> none
    ppermute x4 -> x0, starting transfers between devices: 16.2 us -> none  [the longest x3 14.9 us: per_device(): moving = lax.ppermute(moving, 'col', chain)]
    dot_general x1 -> x0, matrix products: 8.25 us -> none  [dot_exact(): lax.dot_general(left, right, (((contract_left,), (contract_right,)), ((),...]
    unnamed x11 -> x0, local copies, waits for them, and re-layouts: 5.81 us -> none
    slice x3 -> x0, local copies, waits for them, and re-layouts: 3.36 us -> none  [the longest x1 1.26 us: per_device(): own = matrix[:, 0, 0, :]]
  transfers between devices with their start and end apart: 5 -> 0, of which waited for: 3 -> 0; matrix products, arithmetic and copies ran while one was open for 12% -> 0% of each run, Pallas kernels for 0% -> 0%
where the time goes in v2:
time: 88.3 us; the launch traced here: 88.1 us
  Pallas kernels  87.5 us (99%)
    pallas_call x1, Pallas kernels, stream(): pl.pallas_call(functools.partial(stream_kernel, n_row, n_col, owners, chu...  77.3 us
    pallas_call x1, Pallas kernels, update(): pl.pallas_call(functools.partial(update_kernel, 1.0 / math.sqrt(total_row...  10.2 us

profile of v2, /device:TPU:0, one launch (start us, length us, event | category | flops | bytes accessed | tf_op | source)
XLA Modules:
  0.0 88.1 jit_solution(12987216702105693623)
XLA Ops:
  0.6 77.3 %stream.1 = (f32[2,2048,128]{2,1,0:T(8,128)S(1)}, f32[256,640]{1,0:T(8,128)S(1)}, f32[256,256]{1,0:T(8,128)S(1)}) custom-call(f32[2048,5,1,128]{3,2,1,0:T(1,128)} %matrix.3), custom_call_target="tpu_custom_call" | custom-call | tf_op jit(solution)/shard_map/stream/pallas_call | solution.py:455
  77.9 10.2 %update.1 = (f32[256,5,1,128]{3,2,1,0:T(1,128)}, f32[2048,5,1,128]{3,2,1,0:T(1,128)}) custom-call(f32[2048,5,1,128]{3,2,1,0:T(1,128)} %matrix.3, f32[2,2048,128]{2,1,0:T(8,128)S(1)} %get-tuple-element.5.panel, f32[256,640]{1,0:T(8,128)S(1)} %get-tuple-element.6.summed, f32[256,256]{1,0:T(8,128)S(1)} %get-tuple-element.7.inverse), custom_call_target="tpu_custom_call" | custom-call | tf_op jit(solution)/shard_map/update/pallas_call | solution.py:132

commit v3 on v2

--- a/solution.py
+++ b/solution.py
@@ -8,7 +8,8 @@
 from jax.experimental.pallas import tpu as pltpu
 from jax.sharding import PartitionSpec as P
 
-VMEM_LIMIT = 48 * 1024 * 1024
+VMEM_LIMIT = 32 * 1024 * 1024
+STREAM_VMEM_LIMIT = 52 * 1024 * 1024
 LANES = 128
 
 
@@ -67,49 +68,24 @@
 
 
 def update_kernel(
-    scale, chunk, matrix, panel, summed, inverse, r_rows, residual,
-    local, wide, result, top_buf, load_sem, panel_sem, store_sem, top_sem,
+    scale, chunk, local, wide, summed, inverse, r_rows, residual,
+    result, top_buf, store_sem, top_sem,
 ):
-    rows = matrix.shape[0]
-    blocks = matrix.shape[1]
+    blocks, rows = local.shape[0], local.shape[1]
     count = rows // chunk
 
-    def span(c):
-        return pl.ds(c * chunk, chunk)
-
-    def load(c, b):
+    def store(c, b):
+        span = pl.ds(c * chunk, chunk)
         return pltpu.make_async_copy(
-            matrix.at[span(c), b, 0, :], local.at[b, span(c), :], load_sem.at[c, b]
-        )
-
-    def load_panel(c, h):
-        return pltpu.make_async_copy(
-            panel.at[h, span(c), :], wide.at[h, span(c), :], panel_sem.at[c, h]
-        )
-
-    def store(c, b):
-        return pltpu.make_async_copy(
-            result.at[b, span(c), :], residual.at[span(c), b, 0, :], store_sem.at[c, b]
+            result.at[b, span, :], residual.at[span, b, 0, :], store_sem.at[c, b]
         )
 
     def store_top(b):
         return pltpu.make_async_copy(top_buf.at[b], r_rows.at[:, b, 0, :], top_sem.at[b])
 
-    for c in range(count):
-        for h in range(2):
-            load_panel(c, h).start()
-        for b in range(blocks):
-            load(c, b).start()
     top = dot_exact(inverse[...], summed[...], 1, 0)
-    for b in range(blocks):
-        top_buf[b] = top[:, b * LANES : (b + 1) * LANES] * scale
-        store_top(b).start()
     weights = split(dot_exact(inverse[...], top, 0, 0))
     for c in range(count):
-        for h in range(2):
-            load_panel(c, h).wait()
-        for b in range(blocks):
-            load(c, b).wait()
         rows_c = slice(c * chunk, (c + 1) * chunk)
         left = split(jnp.concatenate([wide[0, rows_c, :], wide[1, rows_c, :]], axis=1))
         product = dot_split(left, weights)
@@ -117,43 +93,43 @@
             result[b, rows_c, :] = local[b, rows_c, :] - product[:, b * LANES : (b + 1) * LANES]
             store(c, b).start()
     for b in range(blocks):
+        top_buf[b] = top[:, b * LANES : (b + 1) * LANES] * scale
+        store_top(b).start()
+    for b in range(blocks):
         store_top(b).wait()
         for c in range(count):
             store(c, b).wait()
 
 
-def update(matrix, panel, summed, inverse, total_rows):
-    rows, blocks, _, width = matrix.shape
+def update(local, panel, summed, inverse, total_rows):
+    blocks, rows, width = local.shape
     chunk = 256
     count = rows // chunk
-    names = pltpu.SemaphoreType.DMA
+    sem = pltpu.SemaphoreType.DMA
     vmem = pl.BlockSpec(memory_space=pltpu.VMEM)
     hbm = pl.BlockSpec(memory_space=pl.ANY)
     return pl.pallas_call(
         functools.partial(update_kernel, 1.0 / math.sqrt(total_rows), chunk),
         out_shape=(
             jax.ShapeDtypeStruct((2 * width, blocks, 1, width), jnp.float32),
-            jax.ShapeDtypeStruct(matrix.shape, jnp.float32),
+            jax.ShapeDtypeStruct((rows, blocks, 1, width), jnp.float32),
         ),
-        in_specs=[hbm, hbm, vmem, vmem],
+        in_specs=[vmem] * 4,
         out_specs=(hbm, hbm),
         scratch_shapes=[
             pltpu.VMEM((blocks, rows, width), jnp.float32),
-            pltpu.VMEM((2, rows, width), jnp.float32),
-            pltpu.VMEM((blocks, rows, width), jnp.float32),
             pltpu.VMEM((blocks, 2 * width, width), jnp.float32),
-            names((count, blocks)),
-            names((count, 2)),
-            names((count, blocks)),
-            names((blocks,)),
+            sem((count, blocks)),
+            sem((blocks,)),
         ],
         compiler_params=pltpu.CompilerParams(vmem_limit_bytes=VMEM_LIMIT),
         name="update",
-    )(matrix, panel, summed, inverse)
+    )(local, panel, summed, inverse)
+
 
 def stream_kernel(
-    n_row, n_col, owners, chunk, matrix, panel, summed, inverse,
-    local, wide, work, total, gram, gram_total, slots, gram_slots, factors,
+    n_row, n_col, owners, chunk, matrix, local, panel, summed, inverse,
+    wide, work, total, gram, gram_total, slots, gram_slots, factors,
     load_sem, own_sem, out_sem, recv_sem, send_sem, factor_recv, factor_send,
     scatter_send, scatter_recv, gather_send, gather_recv,
 ):
@@ -201,18 +177,18 @@
 
     def source_of(stage, owner):
         start = pl.multiple_of(owner * piece, 8)
-        if stage == 2:
-            return gram.at[pl.ds(start, piece), :]
+        if stage >= 2:
+            return gram.at[stage - 2, pl.ds(start, piece), :]
         return work.at[pl.ds(stage * LANES + start, piece), :]
 
     def total_of(stage, owner):
         start = pl.multiple_of(owner * piece, 8)
-        if stage == 2:
-            return gram_total.at[pl.ds(start, piece), :]
+        if stage >= 2:
+            return gram_total.at[stage - 2, pl.ds(start, piece), :]
         return total.at[pl.ds(stage * LANES + start, piece), :]
 
     def slot_of(stage, d):
-        return gram_slots.at[d] if stage == 2 else slots.at[stage, d]
+        return gram_slots.at[stage - 2, d] if stage >= 2 else slots.at[stage, d]
 
     def scatter(stage, d):
         owner = lax.rem(row + d, n_row)
@@ -314,120 +290,121 @@
     def _():
         @pl.loop(0, count)
         def _(c):
-            if n_col > 2:
-                send(0, 1, c).start()
+            pl.when(has_right)(send(0, 1, c).start)
             send(1, 1, c).start()
 
     for b in range(blocks):
         load(b).wait()
 
-    @pl.when(col < 2)
+    @pl.when(col == 0)
     def _():
         @pl.loop(0, count)
         def _(c):
-            send(0, 1 - col, c).wait_recv()
-
-            if n_col > 2:
-
-                @pl.when((col == 1) & (c >= count // 2))
-                def _():
-                    send(0, 0, 2 * c - count).start()
-                    send(0, 0, 2 * c - count + 1).start()
-
-            pair = jnp.concatenate([wide[0, span(c), :], wide[1, span(c), :]], axis=1)
-            cross = dot_exact(pair, pair, 0, 0)
-            gram[...] += jnp.concatenate([cross[:LANES], cross[LANES:]], axis=1)
-            work[...] += dot_exact(pair, window(c), 0, 0)
+            mine = wide[0, span(c), :]
+            gram[0, :, :LANES] += dot_exact(mine, mine, 0, 0)
 
         scatter_start(2)
+        scatter_finish(2)
+        gather_finish(2)
+        first = lower_inverse(gram_total[0, :, :LANES])
+        factors[0] = first
+        send_factor(0).start()
+
+        @pl.loop(0, count)
+        def _(c):
+            send(1, 1, c).wait_recv()
+            other = wide[1, span(c), :]
+            pair = jnp.concatenate([wide[0, span(c), :], other], axis=1)
+            gram[1] += dot_exact(other, pair, 0, 0)
+
+        def multiply(start, stop):
+            @pl.loop(start, stop)
+            def _(c):
+                pair = jnp.concatenate([wide[0, span(c), :], wide[1, span(c), :]], axis=1)
+                work[...] += dot_exact(pair, window(c), 0, 0)
+
+        scatter_start(3)
         for half in range(2):
             store_panel(half).start()
+        multiply(0, count // 2)
+        scatter_finish(3)
+        multiply(count // 2, count)
+        gather_finish(3)
         scatter_start(1)
-        scatter_finish(2)
         scatter_start(0)
-        gather_finish(2)
-        first = lower_inverse(gram_total[:, :LANES])
-        factors[0] = first
-
-        if n_col > 2:
-            pl.when(col == 1)(send_factor(0).start)
-        coupling = dot_exact(first, gram_total[:, LANES : 2 * LANES], 1, 0)
-        schur = gram_total[:, 3 * LANES :] - dot_exact(coupling, coupling, 0, 0)
+        coupling = dot_exact(first, gram_total[1, :, :LANES], 1, 1)
+        schur = gram_total[1, :, LANES:] - dot_exact(coupling, coupling, 0, 0)
         carried = dot_exact(coupling, first, 0, 0)
         second = lower_inverse(schur)
         factors[1] = second
-        if n_col > 2:
-            pl.when(col == 1)(send_factor(1).start)
+        send_factor(1).start()
         factors[2] = -dot_exact(second, carried, 1, 0)
-        if n_col > 2:
-            pl.when(col == 1)(send_factor(2).start)
-        scatter_finish(1)
+        send_factor(2).start()
+        for stage in (1, 0):
+            scatter_finish(stage)
+        for stage in (1, 0):
+            gather_finish(stage)
+        for half in range(2):
+            store_panel(half).wait()
+        for stage in range(4):
+            settle(stage)
+
+        @pl.loop(0, count)
+        def _(c):
+            send(0, 0, c).wait_send()
+
+        for which in range(3):
+            send_factor(which).wait_send()
+
+    @pl.when(col >= 1)
+    def _():
+        for half in (1, 0):
+
+            @pl.loop(0, count)
+            def _(c):
+                if half == 1:
+
+                    @pl.when(col >= 2)
+                    def _():
+                        send(0, 1, c).wait_recv()
+                        pl.when(has_right)(send(0, 1, c).start)
+
+                else:
+                    send(0, 0, c).wait_recv()
+                    pl.when(has_right)(send(0, 0, c).start)
+                    pl.when(c == count // 2)(lambda: scatter_finish(1))
+                here = pl.ds(half * LANES, LANES)
+                work[here, :] += dot_exact(wide[half, span(c), :], window(c), 0, 0)
+
+            scatter_start(half)
+            store_panel(half).start()
+
         scatter_finish(0)
+        for which in range(3):
+            send_factor(which).wait_recv()
+            pl.when(has_right)(send_factor(which).start)
         gather_finish(1)
         gather_finish(0)
         for half in range(2):
             store_panel(half).wait()
-        for stage in (2, 1, 0):
+        for stage in (1, 0):
             settle(stage)
 
-        @pl.loop(0, count)
-        def _(c):
-            @pl.when(col == 0)
-            def _():
-                send(0, 0, c).wait_send()
-
-            @pl.when(col == 1)
-            def _():
+        @pl.when(col == 1)
+        def _():
+            @pl.loop(0, count)
+            def _(c):
                 send(1, 1, c).wait_send()
-                if n_col > 2:
-                    send(0, 1, c).wait_send()
-                    send(0, 0, c).wait_send()
-
-        if n_col > 2:
-
-            @pl.when(col == 1)
-            def _():
-                for which in range(3):
-                    send_factor(which).wait_send()
-
-    if n_col > 2:
-
-        @pl.when(col >= 2)
+
+        @pl.when(has_right)
         def _():
-            for half in (1, 0):
-
-                @pl.loop(0, count)
-                def _(c):
-                    send(0, half, c).wait_recv()
-                    pl.when(has_right)(send(0, half, c).start)
-                    if half == 0:
-                        pl.when(c == count // 2)(lambda: scatter_finish(1))
-                    here = pl.ds(half * LANES, LANES)
-                    work[here, :] += dot_exact(wide[half, span(c), :], window(c), 0, 0)
-
-                scatter_start(half)
-                store_panel(half).start()
-
-            scatter_finish(0)
+            @pl.loop(0, count)
+            def _(c):
+                for half in range(2):
+                    send(0, half, c).wait_send()
+
             for which in range(3):
-                send_factor(which).wait_recv()
-                pl.when(has_right)(send_factor(which).start)
-            gather_finish(1)
-            gather_finish(0)
-            for half in range(2):
-                store_panel(half).wait()
-            for stage in (1, 0):
-                settle(stage)
-
-            @pl.when(has_right)
-            def _():
-                @pl.loop(0, count)
-                def _(c):
-                    for half in range(2):
-                        send(0, half, c).wait_send()
-
-                for which in range(3):
-                    send_factor(which).wait_send()
+                send_factor(which).wait_send()
 
     summed[...] = total[...]
     inverse[:LANES, :LANES] = factors[0]
@@ -455,21 +432,21 @@
     return pl.pallas_call(
         functools.partial(stream_kernel, n_row, n_col, owners, chunk),
         out_shape=(
-            jax.ShapeDtypeStruct((2, rows, width), jnp.float32),
+            floats(blocks, rows, width),
+            floats(2, rows, width),
             jax.ShapeDtypeStruct((2 * width, columns), jnp.float32),
             jax.ShapeDtypeStruct((2 * width, 2 * width), jnp.float32),
         ),
         in_specs=[hbm],
-        out_specs=(hbm, vmem, vmem),
+        out_specs=(vmem, vmem, vmem, vmem),
         scratch_shapes=[
-            floats(blocks, rows, width),
             floats(2, rows, width),
             floats(2 * width, columns),
             floats(2 * width, columns),
-            floats(width, 4 * width),
-            floats(width, 4 * width),
+            floats(2, width, 2 * width),
+            floats(2, width, 2 * width),
             floats(2, n_row, piece, columns),
-            floats(n_row, piece, 4 * width),
+            floats(2, n_row, piece, 2 * width),
             floats(3, width, width),
             sem((blocks,)),
             sem,
@@ -478,22 +455,22 @@
             sem((2, 2, count)),
             sem((3,)),
             sem((3,)),
-            sem((3, n_row)),
-            sem((3, n_row)),
-            sem((3, n_row)),
-            sem((3, n_row)),
+            sem((4, n_row)),
+            sem((4, n_row)),
+            sem((4, n_row)),
+            sem((4, n_row)),
         ],
         compiler_params=pltpu.CompilerParams(
-            collective_id=0, has_side_effects=True, vmem_limit_bytes=VMEM_LIMIT
+            collective_id=0, has_side_effects=True, vmem_limit_bytes=STREAM_VMEM_LIMIT
         ),
         name="stream",
     )(matrix)
 
 
 def per_device(matrix):
-    panel, summed, inverse = stream(matrix)
+    local, panel, summed, inverse = stream(matrix)
     total_rows = matrix.shape[0] * lax.axis_size("row")
-    return update(matrix, panel, summed, inverse, total_rows)
+    return update(local, panel, summed, inverse, total_rows)
 
 
 def solution(mesh):

time: 88.3 us -> 75.4 us (0.85)
  the two profiles are of different devices: /device:TPU:0 before, /device:TPU:27 now
where the time goes in v3:
time: 75.4 us; the launch traced here: 75.2 us
  Pallas kernels  72.6 us (96%)
  local copies, waits for them, and re-layouts  2.03 us (3%)
    pallas_call x1, Pallas kernels, stream(): pl.pallas_call(functools.partial(stream_kernel, n_row, n_col, owners, chu...  66.9 us
    pallas_call x1, Pallas kernels, update(): pl.pallas_call(functools.partial(update_kernel, 1.0 / math.sqrt(total_row...  5.67 us
    unnamed x4, local copies, waits for them, and re-layouts  2.03 us

profile of v3, /device:TPU:27, one launch (start us, length us, event | category | flops | bytes accessed | tf_op | source)
XLA Modules:
  0.0 75.2 jit_solution(14662561412986240051)
XLA Ops:
  0.6 66.9 %stream.1 = (f32[5,2048,128]{2,1,0:T(8,128)S(1)}, f32[2,2048,128]{2,1,0:T(8,128)S(1)}, f32[256,640]{1,0:T(8,128)}, f32[256,256]{1,0:T(8,128)}) custom-call(f32[2048,5,1,128]{3,2,1,0:T(1,128)} %matrix.1), custom_call_target="tpu_custom_call" | custom-call | tf_op jit(solution)/shard_map/stream/pallas_call | solution.py:432
  67.5 0.0 copy-start
  67.5 1.1 %copy-done = f32[256,640]{1,0:T(8,128)S(1)} copy-done((f32[256,640]{1,0:T(8,128)S(1)}, f32[256,640]{1,0:T(8,128)}, u32[]{:S(2)}) %copy-start) | copy-done | bytes 655384
  68.6 0.0 copy-start.1
  68.6 0.9 %copy-done.1 = f32[256,256]{1,0:T(8,128)S(1)} copy-done((f32[256,256]{1,0:T(8,128)S(1)}, f32[256,256]{1,0:T(8,128)}, u32[]{:S(2)}) %copy-start.1) | copy-done | bytes 262168
  69.6 5.7 %update.1 = (f32[256,5,1,128]{3,2,1,0:T(1,128)}, f32[2048,5,1,128]{3,2,1,0:T(1,128)}) custom-call(f32[5,2048,128]{2,1,0:T(8,128)S(1)} %get-tuple-element.6.local, f32[2,2048,128]{2,1,0:T(8,128)S(1)} %get-tuple-element.7.wide, f32[256,640]{1,0:T(8,128)S(1)} %copy-done, f32[256,256]{1,0:T(8,128)S(1)} %copy-done.1), custom_call_target="tpu_custom_call" | custom-call | tf_op jit(solution)/shard_map/update/pallas_call | solution.py:111
Async XLA Ops:
  67.5 1.1 %copy-start = (f32[256,640]{1,0:T(8,128)S(1)}, f32[256,640]{1,0:T(8,128)}, u32[]{:S(2)}) copy-start(f32[256,640]{1,0:T(8,128)} %get-tuple-element.8.summed) | copy-start | bytes 1966084
  68.6 0.9 %copy-start.1 = (f32[256,256]{1,0:T(8,128)S(1)}, f32[256,256]{1,0:T(8,128)}, u32[]{:S(2)}) copy-start(f32[256,256]{1,0:T(8,128)} %get-tuple-element.9.inverse) | copy-start | bytes 786436
